TPU v7x, 32 devices: a whole 2x2x4 slice. The times are simulated.
32 devices in a mesh: tm: 4 (over x, core), pts: 8 (over z, y).
Axes of the slice: x: 2, y: 2, z: 4, core: 2. Of those that a mesh axis runs over, the one named last changes fastest.
Arguments:
- base_grid: float32 [12, 128, 8192], P(None, 'tm', 'pts'), may hold values from -5 to 5
- sample_index: int32 [4096], P('pts'), may hold values from 0 to 1023, as said below
- exponents: int32 [512, 12], replicated, may hold values from 0 to 3, as said below
Outputs:
- gram: float32 [512, 512], P('pts', 'tm')
- cross: float32 [3, 512], P(None, 'pts')
Inputs may be any that keep to these rules, and one draw needn't show every extreme that they name: `sample_index`: within one index of pts the sampled cells are distinct, and each is below 1024. `exponents`: every term has total degree at most 3.
All inputs are finite; a program needn't handle non-finite values.
Results may differ from a plain program's by a relative error of at most 0.00034.
Values sent between devices are 32-bit elements; how exact they have to be, the bound alone decides.
A program may use at most 192 MiB of HBM per device.

v0:
```python
import jax
import jax.numpy as jnp
from jax import lax
from jax.sharding import PartitionSpec as P


def passed_along(value, axis, by):
    size = lax.axis_size(axis)
    pairs = [(i, i + by) for i in range(size) if 0 <= i + by < size]
    return lax.ppermute(value, axis, pairs)


def broadcast(value, axis, source):
    kept = jnp.where(lax.axis_index(axis) == source, value, 0).astype(value.dtype)
    return lax.psum(kept, axis)


def monomials(piece, exponents):
    theta = jnp.ones((exponents.shape[0],) + piece.shape[1:], jnp.float32)
    for field in range(piece.shape[0]):
        value = piece[field][None]
        square = value * value
        power = exponents[:, field][:, None, None]
        factor = jnp.where(
            power == 0,
            jnp.float32(1.0),
            jnp.where(power == 1, value, jnp.where(power == 2, square, square * value)),
        )
        theta = theta * factor
    return theta


def products(source, earlier, initial, exponents, scale, targets):
    snaps = source.shape[1]
    points = source.shape[2]
    terms = exponents.shape[0]
    width = min(64, points)
    count = points // width

    def add_products(number, carry):
        gram_acc, cross_acc = carry
        piece = lax.dynamic_slice_in_dim(source, number * width, width, 2)
        theta = monomials(piece, exponents)
        running = jnp.cumsum(theta, axis=1)
        before = jnp.concatenate([jnp.zeros_like(running[:, :1]), running[:, :-1]], axis=1)
        offset = lax.dynamic_slice_in_dim(earlier, number * width, width, 1)
        integral = (
            ((before + offset[:, None, :]) * scale)
            .astype(jnp.bfloat16)
            .reshape(terms, snaps * width)
        )
        first = lax.dynamic_slice_in_dim(initial, number * width, width, 1)
        increment = (
            (piece[:targets] - first[:, None, :])
            .astype(jnp.bfloat16)
            .reshape(targets, snaps * width)
        )
        contract = (((1,), (1,)), ((), ()))
        gram_acc = gram_acc + lax.dot_general(
            integral, integral, contract, preferred_element_type=jnp.float32
        )
        cross_acc = cross_acc + lax.dot_general(
            increment, integral, contract, preferred_element_type=jnp.float32
        )
        return (gram_acc, cross_acc)

    start = (jnp.zeros((terms, terms), jnp.float32), jnp.zeros((targets, terms), jnp.float32))
    return lax.fori_loop(0, count, add_products, start)


def shards(base_grid, sample_index, exponents):
    fields, snaps, unused_cells = base_grid.shape
    points = sample_index.shape[0]
    terms = exponents.shape[0]
    targets = 3
    time_devices = lax.axis_size("tm")
    point_devices = lax.axis_size("pts")
    sampled = jnp.take(base_grid, sample_index, axis=2)
    width = min(64, points)
    count = points // width
    scale = jnp.float32(1.0 / (snaps * time_devices))

    def add_totals(number, totals):
        piece = lax.dynamic_slice_in_dim(sampled, number * width, width, 2)
        theta = monomials(piece, exponents)
        return lax.dynamic_update_slice_in_dim(totals, jnp.sum(theta, axis=1), number * width, 1)

    totals = lax.fori_loop(0, count, add_totals, jnp.zeros((terms, points), jnp.float32))
    earlier = jnp.zeros_like(totals)
    for hop in range(time_devices - 1):
        earlier = passed_along(earlier + totals, "tm", 1)
    initial = broadcast(sampled[:targets, 0, :], "tm", 0)
    gram_part, cross_part = products(sampled, earlier, initial, exponents, scale, targets)
    norm = jnp.float32(1.0 / (snaps * time_devices * points * point_devices))
    row_span = terms // point_devices
    col_span = terms // time_devices
    gram_full, cross_full = lax.psum((gram_part, cross_part), ("tm", "pts"))
    row_start = lax.axis_index("pts") * row_span
    col_start = lax.axis_index("tm") * col_span
    gram_own = lax.dynamic_slice(gram_full, (row_start, col_start), (row_span, col_span))
    cross_own = lax.dynamic_slice_in_dim(cross_full, row_start, row_span, 1)
    return (gram_own * norm, cross_own * norm)


def solution(mesh):
    return jax.shard_map(
        shards,
        mesh=mesh,
        in_specs=(P(None, "tm", "pts"), P("pts"), P()),
        out_specs=(P("pts", "tm"), P(None, "pts")),
        check_vma=False,
    )
```

profile of v0, /device:TPU:0, one launch (start us, length us, event | category | flops | bytes accessed | tf_op | source)
XLA Modules:
  0.0 638.6 jit_solution(905357390255151748)
XLA Ops:
  8.6 7.2 %copy.23 = f32[12,32,1024]{1,0,2:T(8,128)} copy(f32[12,32,1024]{2,1,0:T(8,128)} %param.7) | data formatting | bytes 3145728 | tf_op args[0]
  29.9 166.2 %while.29 = (s32[]{:T(128)}, f32[512,512]{0,1:T(8,128)S(1)}, s32[512,12]{0,1:T(8,128)S(1)}, f32[12,32,512]{2,1,0:T(8,128)S(1)}, s32[]{:T(128)}, /*index=5*/s32[]...) while((s32[]{:T(128)}, f32[512,512]{0,1:T(8,128)S(1)}, ...), condition=%wide.region_2.3_spmd, body=%wide.region_0.0_spmd.sunk | while | flops 50366480 | bytes 1159571 | solution.py:88
  30.3 20.3 %multiply_reduce_fusion.2 = f32[512,64]{0,1:T(8,128)S(1)} fusion(f32[32,64]{1,0:T(8,128)S(1)} %get-tuple-element.687, f32[32,64]{1,0:T(8,128)S(1)} %get-tuple-element.688, f32[32,64]{1,0:T(8,128)S(1)} %get-tuple-element.689, f32[32,64]{1,0:T(8,128)S(1)} %get-tuple-element.690, f32[32,64]{1,0:T(8,128)S(1)} %get-tuple-element.691, ...), kind=kLoop, calls=%fused_computation.1.clone.1 | loop fusion | flops 50298880 | bytes 444416 | tf_op jit(solution)/shard_map/while/body/eval_jaxpr/reduce_sum | solution.py:86
  51.1 20.3 %multiply_reduce_fusion.2 = f32[512,64]{0,1:T(8,128)S(1)} fusion(f32[32,64]{1,0:T(8,128)S(1)} %get-tuple-element.687, f32[32,64]{1,0:T(8,128)S(1)} %get-tuple-element.688, f32[32,64]{1,0:T(8,128)S(1)} %get-tuple-element.689, f32[32,64]{1,0:T(8,128)S(1)} %get-tuple-element.690, f32[32,64]{1,0:T(8,128)S(1)} %get-tuple-element.691, ...), kind=kLoop, calls=%fused_computation.1.clone.1 | loop fusion | flops 50298880 | bytes 444416 | tf_op jit(solution)/shard_map/while/body/eval_jaxpr/reduce_sum | solution.py:86
  71.9 20.3 %multiply_reduce_fusion.2 = f32[512,64]{0,1:T(8,128)S(1)} fusion(f32[32,64]{1,0:T(8,128)S(1)} %get-tuple-element.687, f32[32,64]{1,0:T(8,128)S(1)} %get-tuple-element.688, f32[32,64]{1,0:T(8,128)S(1)} %get-tuple-element.689, f32[32,64]{1,0:T(8,128)S(1)} %get-tuple-element.690, f32[32,64]{1,0:T(8,128)S(1)} %get-tuple-element.691, ...), kind=kLoop, calls=%fused_computation.1.clone.1 | loop fusion | flops 50298880 | bytes 444416 | tf_op jit(solution)/shard_map/while/body/eval_jaxpr/reduce_sum | solution.py:86
  92.6 20.3 %multiply_reduce_fusion.2 = f32[512,64]{0,1:T(8,128)S(1)} fusion(f32[32,64]{1,0:T(8,128)S(1)} %get-tuple-element.687, f32[32,64]{1,0:T(8,128)S(1)} %get-tuple-element.688, f32[32,64]{1,0:T(8,128)S(1)} %get-tuple-element.689, f32[32,64]{1,0:T(8,128)S(1)} %get-tuple-element.690, f32[32,64]{1,0:T(8,128)S(1)} %get-tuple-element.691, ...), kind=kLoop, calls=%fused_computation.1.clone.1 | loop fusion | flops 50298880 | bytes 444416 | tf_op jit(solution)/shard_map/while/body/eval_jaxpr/reduce_sum | solution.py:86
  113.4 20.3 %multiply_reduce_fusion.2 = f32[512,64]{0,1:T(8,128)S(1)} fusion(f32[32,64]{1,0:T(8,128)S(1)} %get-tuple-element.687, f32[32,64]{1,0:T(8,128)S(1)} %get-tuple-element.688, f32[32,64]{1,0:T(8,128)S(1)} %get-tuple-element.689, f32[32,64]{1,0:T(8,128)S(1)} %get-tuple-element.690, f32[32,64]{1,0:T(8,128)S(1)} %get-tuple-element.691, ...), kind=kLoop, calls=%fused_computation.1.clone.1 | loop fusion | flops 50298880 | bytes 444416 | tf_op jit(solution)/shard_map/while/body/eval_jaxpr/reduce_sum | solution.py:86
  134.2 20.3 %multiply_reduce_fusion.2 = f32[512,64]{0,1:T(8,128)S(1)} fusion(f32[32,64]{1,0:T(8,128)S(1)} %get-tuple-element.687, f32[32,64]{1,0:T(8,128)S(1)} %get-tuple-element.688, f32[32,64]{1,0:T(8,128)S(1)} %get-tuple-element.689, f32[32,64]{1,0:T(8,128)S(1)} %get-tuple-element.690, f32[32,64]{1,0:T(8,128)S(1)} %get-tuple-element.691, ...), kind=kLoop, calls=%fused_computation.1.clone.1 | loop fusion | flops 50298880 | bytes 444416 | tf_op jit(solution)/shard_map/while/body/eval_jaxpr/reduce_sum | solution.py:86
  155.0 20.3 %multiply_reduce_fusion.2 = f32[512,64]{0,1:T(8,128)S(1)} fusion(f32[32,64]{1,0:T(8,128)S(1)} %get-tuple-element.687, f32[32,64]{1,0:T(8,128)S(1)} %get-tuple-element.688, f32[32,64]{1,0:T(8,128)S(1)} %get-tuple-element.689, f32[32,64]{1,0:T(8,128)S(1)} %get-tuple-element.690, f32[32,64]{1,0:T(8,128)S(1)} %get-tuple-element.691, ...), kind=kLoop, calls=%fused_computation.1.clone.1 | loop fusion | flops 50298880 | bytes 444416 | tf_op jit(solution)/shard_map/while/body/eval_jaxpr/reduce_sum | solution.py:86
  175.7 20.3 %multiply_reduce_fusion.2 = f32[512,64]{0,1:T(8,128)S(1)} fusion(f32[32,64]{1,0:T(8,128)S(1)} %get-tuple-element.687, f32[32,64]{1,0:T(8,128)S(1)} %get-tuple-element.688, f32[32,64]{1,0:T(8,128)S(1)} %get-tuple-element.689, f32[32,64]{1,0:T(8,128)S(1)} %get-tuple-element.690, f32[32,64]{1,0:T(8,128)S(1)} %get-tuple-element.691, ...), kind=kLoop, calls=%fused_computation.1.clone.1 | loop fusion | flops 50298880 | bytes 444416 | tf_op jit(solution)/shard_map/while/body/eval_jaxpr/reduce_sum | solution.py:86
  200.9 14.0 %collective-permute-start.1 = (f32[512,512]{0,1:T(8,128)S(1)}, f32[512,512]{0,1:T(8,128)S(1)}, u32[]{:S(2)}, u32[]{:S(2)}) collective-permute-start(f32[512,512]{0,1:T(8,128)S(1)} %add.114), channel_id=1, source_target_pairs={{0,8},{8,16},{16,24},{1,9},{9,17},{17,25},{2,10},{10,18},{18,26},{... | collective-permute-start | bytes 3145736 | tf_op jit(solution)/shard_map/ppermute | solution.py:10
  217.3 14.8 %collective-permute-start.2 = (f32[512,512]{0,1:T(8,128)S(1)}, f32[512,512]{0,1:T(8,128)}, u32[]{:S(2)}, u32[]{:S(2)}) collective-permute-start(f32[512,512]{0,1:T(8,128)S(1)} %add.115), channel_id=1, source_target_pairs={{0,8},{8,16},{16,24},{1,9},{9,17},{17,25},{2,10},{10,18},{18,26},{... | collective-permute-start | bytes 3145736 | tf_op jit(solution)/shard_map/ppermute | solution.py:10
  237.6 7.8 %psum.21 = f32[3,512]{1,0:T(4,128)S(1)} all-reduce(f32[3,512]{1,0:T(4,128)S(1)} %bitcast.317), channel_id=1, replica_groups=mesh['tm'=4,'pts'=8] {'tm'}, use_global_device_ids=true, to_apply=%region_3.4 | all-reduce | flops 1536 | bytes 12288 | tf_op jit(solution)/shard_map/psum | solution.py:15
  245.4 251.2 %while.30 = (s32[]{:T(128)}, f32[512,512]{1,0:T(8,128)}, f32[3,512]{1,0:T(4,128)S(1)}, s32[512,12]{0,1:T(8,128)S(1)}, f32[12,32,512]{2,0,1:T(8,128)S(1)}, /*inde...) while((s32[]{:T(128)}, f32[512,512]{1,0:T(8,128)}, ...), condition=%wide.region_6.7_spmd.clone, body=%wide.region_4.6_spmd.clone.sunk | while | flops 1168745472 | bytes 48658448 | solution.py:68
  246.5 21.3 %fusion.165 = f32[512,32,64]{0,2,1:T(8,128)S(1)} fusion(f32[32,64]{1,0:T(8,128)S(1)} %bitcast.315, f32[32,64]{1,0:T(8,128)S(1)} %bitcast.294, f32[32,64]{1,0:T(8,128)S(1)} %bitcast.272, f32[32,64]{1,0:T(8,128)S(1)} %bitcast.316, f32[32,64]{1,0:T(8,128)S(1)} %bitcast.295, f32[32,64]{1,0:T(8,128)S(1)} %bitcast.274, f32[32,64]{1,0:T(8,128)S(1)} %bitcast.313, ...), kind=kOutput, calls=%fused_computation.88.clone.1 | output fusion | flops 81788928 | bytes 4507648 | tf_op jit(solution)/shard_map/while/body/eval_jaxpr/jit(cumsum)/reduce_window_sum | solution.py:44
  277.9 21.3 %fusion.165 = f32[512,32,64]{0,2,1:T(8,128)S(1)} fusion(f32[32,64]{1,0:T(8,128)S(1)} %bitcast.315, f32[32,64]{1,0:T(8,128)S(1)} %bitcast.294, f32[32,64]{1,0:T(8,128)S(1)} %bitcast.272, f32[32,64]{1,0:T(8,128)S(1)} %bitcast.316, f32[32,64]{1,0:T(8,128)S(1)} %bitcast.295, f32[32,64]{1,0:T(8,128)S(1)} %bitcast.274, f32[32,64]{1,0:T(8,128)S(1)} %bitcast.313, ...), kind=kOutput, calls=%fused_computation.88.clone.1 | output fusion | flops 81788928 | bytes 4507648 | tf_op jit(solution)/shard_map/while/body/eval_jaxpr/jit(cumsum)/reduce_window_sum | solution.py:44
  309.3 21.3 %fusion.165 = f32[512,32,64]{0,2,1:T(8,128)S(1)} fusion(f32[32,64]{1,0:T(8,128)S(1)} %bitcast.315, f32[32,64]{1,0:T(8,128)S(1)} %bitcast.294, f32[32,64]{1,0:T(8,128)S(1)} %bitcast.272, f32[32,64]{1,0:T(8,128)S(1)} %bitcast.316, f32[32,64]{1,0:T(8,128)S(1)} %bitcast.295, f32[32,64]{1,0:T(8,128)S(1)} %bitcast.274, f32[32,64]{1,0:T(8,128)S(1)} %bitcast.313, ...), kind=kOutput, calls=%fused_computation.88.clone.1 | output fusion | flops 81788928 | bytes 4507648 | tf_op jit(solution)/shard_map/while/body/eval_jaxpr/jit(cumsum)/reduce_window_sum | solution.py:44
  340.6 21.3 %fusion.165 = f32[512,32,64]{0,2,1:T(8,128)S(1)} fusion(f32[32,64]{1,0:T(8,128)S(1)} %bitcast.315, f32[32,64]{1,0:T(8,128)S(1)} %bitcast.294, f32[32,64]{1,0:T(8,128)S(1)} %bitcast.272, f32[32,64]{1,0:T(8,128)S(1)} %bitcast.316, f32[32,64]{1,0:T(8,128)S(1)} %bitcast.295, f32[32,64]{1,0:T(8,128)S(1)} %bitcast.274, f32[32,64]{1,0:T(8,128)S(1)} %bitcast.313, ...), kind=kOutput, calls=%fused_computation.88.clone.1 | output fusion | flops 81788928 | bytes 4507648 | tf_op jit(solution)/shard_map/while/body/eval_jaxpr/jit(cumsum)/reduce_window_sum | solution.py:44
  372.0 21.3 %fusion.165 = f32[512,32,64]{0,2,1:T(8,128)S(1)} fusion(f32[32,64]{1,0:T(8,128)S(1)} %bitcast.315, f32[32,64]{1,0:T(8,128)S(1)} %bitcast.294, f32[32,64]{1,0:T(8,128)S(1)} %bitcast.272, f32[32,64]{1,0:T(8,128)S(1)} %bitcast.316, f32[32,64]{1,0:T(8,128)S(1)} %bitcast.295, f32[32,64]{1,0:T(8,128)S(1)} %bitcast.274, f32[32,64]{1,0:T(8,128)S(1)} %bitcast.313, ...), kind=kOutput, calls=%fused_computation.88.clone.1 | output fusion | flops 81788928 | bytes 4507648 | tf_op jit(solution)/shard_map/while/body/eval_jaxpr/jit(cumsum)/reduce_window_sum | solution.py:44
  403.4 21.3 %fusion.165 = f32[512,32,64]{0,2,1:T(8,128)S(1)} fusion(f32[32,64]{1,0:T(8,128)S(1)} %bitcast.315, f32[32,64]{1,0:T(8,128)S(1)} %bitcast.294, f32[32,64]{1,0:T(8,128)S(1)} %bitcast.272, f32[32,64]{1,0:T(8,128)S(1)} %bitcast.316, f32[32,64]{1,0:T(8,128)S(1)} %bitcast.295, f32[32,64]{1,0:T(8,128)S(1)} %bitcast.274, f32[32,64]{1,0:T(8,128)S(1)} %bitcast.313, ...), kind=kOutput, calls=%fused_computation.88.clone.1 | output fusion | flops 81788928 | bytes 4507648 | tf_op jit(solution)/shard_map/while/body/eval_jaxpr/jit(cumsum)/reduce_window_sum | solution.py:44
  434.7 21.3 %fusion.165 = f32[512,32,64]{0,2,1:T(8,128)S(1)} fusion(f32[32,64]{1,0:T(8,128)S(1)} %bitcast.315, f32[32,64]{1,0:T(8,128)S(1)} %bitcast.294, f32[32,64]{1,0:T(8,128)S(1)} %bitcast.272, f32[32,64]{1,0:T(8,128)S(1)} %bitcast.316, f32[32,64]{1,0:T(8,128)S(1)} %bitcast.295, f32[32,64]{1,0:T(8,128)S(1)} %bitcast.274, f32[32,64]{1,0:T(8,128)S(1)} %bitcast.313, ...), kind=kOutput, calls=%fused_computation.88.clone.1 | output fusion | flops 81788928 | bytes 4507648 | tf_op jit(solution)/shard_map/while/body/eval_jaxpr/jit(cumsum)/reduce_window_sum | solution.py:44
  466.1 21.3 %fusion.165 = f32[512,32,64]{0,2,1:T(8,128)S(1)} fusion(f32[32,64]{1,0:T(8,128)S(1)} %bitcast.315, f32[32,64]{1,0:T(8,128)S(1)} %bitcast.294, f32[32,64]{1,0:T(8,128)S(1)} %bitcast.272, f32[32,64]{1,0:T(8,128)S(1)} %bitcast.316, f32[32,64]{1,0:T(8,128)S(1)} %bitcast.295, f32[32,64]{1,0:T(8,128)S(1)} %bitcast.274, f32[32,64]{1,0:T(8,128)S(1)} %bitcast.313, ...), kind=kOutput, calls=%fused_computation.88.clone.1 | output fusion | flops 81788928 | bytes 4507648 | tf_op jit(solution)/shard_map/while/body/eval_jaxpr/jit(cumsum)/reduce_window_sum | solution.py:44
  496.6 42.6 %psum.23 = f32[3,512]{1,0:T(4,128)S(1)} all-reduce(f32[3,512]{1,0:T(4,128)S(1)} %get-tuple-element.208), channel_id=1, replica_groups=mesh['tm'=4,'pts'=8] {'tm','pts'}, use_global_device_ids=true, to_apply=%region_8.9 | all-reduce | flops 1536 | bytes 12288 | tf_op jit(solution)/shard_map/psum | solution.py:97
  539.9 90.4 %all-reduce.3.cloned.1.call-done = f32[512,512]{1,0:T(8,128)} async-done(((f32[512,512]{1,0:T(8,128)}), f32[512,512]{1,0:T(8,128)}) %all-reduce.3.cloned.1.call-update) | async-done | bytes 1048592 | tf_op jit(solution)/shard_map/psum | solution.py:97
  (216 shorter events, 113.5 us)
Async XLA Ops:
  7.2 623.2 %all-reduce.3.cloned.1.call-start = ((), (), s32[]{:S(2)}) async-start(), calls=%async_computation | async-start | bytes 2097152 | tf_op jit(solution)/shard_map/psum | solution.py:97
  26.7 3.2 copy-start.1
  196.0 4.6 collective-permute-start
  200.9 16.2 %collective-permute-start.1 = (f32[512,512]{0,1:T(8,128)S(1)}, f32[512,512]{0,1:T(8,128)S(1)}, u32[]{:S(2)}, u32[]{:S(2)}) collective-permute-start(f32[512,512]{0,1:T(8,128)S(1)} %add.114), channel_id=1, source_target_pairs={{0,8},{8,16},{16,24},{1,9},{9,17},{17,25},{2,10},{10,18},{18,26},{... | collective-permute-start | bytes 3145736 | tf_op jit(solution)/shard_map/ppermute | solution.py:10
  217.3 28.1 %collective-permute-start.2 = (f32[512,512]{0,1:T(8,128)S(1)}, f32[512,512]{0,1:T(8,128)}, u32[]{:S(2)}, u32[]{:S(2)}) collective-permute-start(f32[512,512]{0,1:T(8,128)S(1)} %add.115), channel_id=1, source_target_pairs={{0,8},{8,16},{16,24},{1,9},{9,17},{17,25},{2,10},{10,18},{18,26},{... | collective-permute-start | bytes 3145736 | tf_op jit(solution)/shard_map/ppermute | solution.py:10
  267.8 3.3 copy-start.2
  271.1 5.0 copy-start
  299.2 3.3 copy-start.2
  302.5 5.0 copy-start
  307.4 1.0 copy-start.3
  330.5 3.3 copy-start.2
  333.9 5.0 copy-start
  338.8 1.0 copy-start.3
  361.9 3.3 copy-start.2
  365.2 5.0 copy-start
  393.3 3.3 copy-start.2
  396.6 5.0 copy-start
  424.7 3.3 copy-start.2
  428.0 5.0 copy-start
  432.9 1.0 copy-start.3
  456.0 3.3 copy-start.2
  459.4 5.0 copy-start
  487.4 3.3 copy-start.2
  490.7 5.0 copy-start
  (5 other events, 4.9 us)
Sparse Core Ops, SparseCore 0:
  496.8 133.5 all-reduce.2
where the time goes:
time: 639 us
  other arithmetic  352 us (55%)
  waiting for transfers between devices  94.8 us (15%)
  blocking collectives  50.5 us (8%)
  local copies, waits for them, and re-layouts  49.4 us (8%)
  matrix products  44.3 us (7%)
  starting transfers between devices  31.3 us (5%)
  between operations  14.1 us (2%)
    another operation x8, other arithmetic, add_products(): running = jnp.cumsum(theta, axis=1)  170 us
    reduce_sum x8, other arithmetic, add_totals(): jnp.sum(theta, axis=1)  162 us
    psum x1, waiting for transfers between devices, shards(): gram_full, cross_full = lax.psum((gram_part, cross_part), ('tm', 'pts'))  90.4 us
    psum x1, blocking collectives, shards(): gram_full, cross_full = lax.psum((gram_part, cross_part), ('tm', 'pts'))  42.6 us
    dot_general x8, matrix products, add_products(): lax.dot_general(integral, integral, contract, preferred_element_type=jnp....  39 us
    ppermute x3, starting transfers between devices, passed_along(): return lax.ppermute(value, axis, pairs)  31.3 us
    slice x8, local copies, waits for them, and re-layouts, add_products(): running[:, :-1]  19.1 us
  transfers between devices with their start and end apart: 4, of which 3 were waited for; matrix products, arithmetic and copies ran while one was open for 1% of the time, Pallas kernels for 0%

commit v1 on v0

v1 whole, which is shorter than its diff:
```python
import itertools

import jax
import jax.numpy as jnp
import numpy as np
from jax import lax
from jax.experimental import pallas as pl
from jax.experimental.pallas import tpu as pltpu
from jax.sharding import PartitionSpec as P

LANES = 128
SLOTS = 16
TARGETS = 3
BLOCK = 8
F32 = jnp.float32
BF16 = jnp.bfloat16


def nt(a, b):
    return lax.dot_general(a, b, (((1,), (1,)), ((), ())), preferred_element_type=F32)


def split_two(value):
    high = value.astype(BF16)
    return high, (value - high.astype(F32)).astype(BF16)


def row_plan():
    plan, labels = [], []
    a_rows = {r: [(i + r) % 8 for i in range(8)] for r in range(8)}
    slot_var = [8, 9, 10, 11, 12, 8, 9, 10]
    b_rows = {r: [slot_var[(i + r) % 8] for i in range(8)] for r in range(8)}

    def add(kind, factors):
        plan.append(kind)
        labels.append([tuple(sorted(row)) for row in zip(*factors)])

    for r in range(5):
        for b in range(5):
            add(("aab", r, b), (a_rows[0], a_rows[r], [8 + b] * 8))
    for i in range(5):
        for j in range(i, 5):
            add(("abb", i, j), (a_rows[0], [8 + i] * 8, [8 + j] * 8))
    seen = set()
    for r in range(5):
        for s in range(8):
            rows = [tuple(sorted(row)) for row in zip(a_rows[0], a_rows[r], a_rows[s])]
            if not seen.intersection(rows):
                seen.update(rows)
                add(("aaa", r, s), (a_rows[0], a_rows[r], a_rows[s]))
    for i, j, k in ((0, 0, 0), (0, 0, 1), (0, 0, 2), (0, 0, 3), (1, 1, 0), (0, 1, 2), (0, 1, 3)):
        add(("bbb", i, j, k), (b_rows[i], b_rows[j], b_rows[k]))
    codes, known = [], set()
    for label in itertools.chain(*labels):
        fresh = label not in known
        known.add(label)
        codes.append(float(sum(4**v for v in label if v < 12)) if fresh else -1.0)
    assert len(known) == 455
    return plan, codes


PLAN, CODES = row_plan()
ROWS = 8 * len(PLAN)
FULL = -(-(ROWS + 8) // 16) * 16
HALF = FULL // 2


def sample(grid_ref, index_ref, out_ref):
    cells = grid_ref.shape[1]
    width = index_ref.shape[1]
    number = lax.broadcasted_iota(jnp.int32, (cells, width), 0)
    hot = jnp.where(number == index_ref[...], 1.0, 0.0).astype(BF16)
    value = grid_ref[...]
    high, rest = value.astype(BF16), None
    rest = value - high.astype(F32)
    middle, low = split_two(rest)
    out = jnp.dot(high, hot, preferred_element_type=F32)
    out += jnp.dot(middle, hot, preferred_element_type=F32)
    out += jnp.dot(low, hot, preferred_element_type=F32)
    for d in range(out_ref.shape[0]):
        out_ref[d] = out[:, d * LANES : (d + 1) * LANES]


def build(xs, first, run, integral, source, start, snaps):
    for sub in range(0, BLOCK, 4):
        steps = range(4)
        v, quad, wide = [], [], []
        for j in steps:
            t = start + sub + j
            v.append(xs[source, pl.ds(t, 8, stride=snaps), :])
            quad.append({})
            wide.append(
                [
                    jnp.broadcast_to(xs[source, pl.ds((8 + b) * snaps + t, 1), :], (8, LANES))
                    for b in range(5)
                ]
            )

        def rolled(j, r):
            return v[j] if r == 0 else pltpu.roll(v[j], 8 - r, 0)

        def pair(j, r):
            if r not in quad[j]:
                quad[j][r] = v[j] * rolled(j, r)
            return quad[j][r]

        def b_window(j, r):
            w = xs[source, pl.ds(8 * snaps + start + sub + j, 8, stride=snaps), :]
            return w if r == 0 else pltpu.roll(w, 8 - r, 0)

        def theta(kind, j):
            if kind[0] == "aab":
                return pair(j, kind[1]) * wide[j][kind[2]]
            if kind[0] == "abb":
                return (v[j] * wide[j][kind[1]]) * wide[j][kind[2]]
            if kind[0] == "aaa":
                return pair(j, kind[1]) * rolled(j, kind[2])
            return (b_window(j, kind[1]) * b_window(j, kind[2])) * b_window(j, kind[3])

        for g in range(0, len(PLAN), 2):
            rows = slice(8 * g, 8 * g + 16)
            now = run[rows, :]
            for j in steps:
                lanes = slice((sub + j) * LANES, (sub + j + 1) * LANES)
                integral[rows, lanes] = now.astype(BF16)
                now = now + jnp.concatenate([theta(PLAN[g], j), theta(PLAN[g + 1], j)], 0)
            run[rows, :] = now
        for j in steps:
            lanes = slice((sub + j) * LANES, (sub + j + 1) * LANES)
            change = v[j] - first
            both = jnp.concatenate([change, jnp.zeros_like(change)], 0)
            integral[ROWS : ROWS + 16, lanes] = both.astype(BF16)


def add_products(integral, g00, g01, g11):
    top, bottom = integral[:HALF, :], integral[HALF:, :]
    g00[...] += nt(top, top)
    g01[...] += nt(top, bottom)
    g11[...] += nt(bottom, bottom)


def chosen(exps_ref, codes_ref, g00, g01, g11):
    terms, fields = exps_ref.shape
    power = lax.broadcasted_iota(jnp.int32, (1, fields), 1)
    weight = lax.shift_left(jnp.int32(1), 2 * power).astype(F32)
    code = jnp.sum(exps_ref[...].astype(F32) * weight, axis=1, keepdims=True)
    pick = jnp.where(code == codes_ref[...], 1.0, 0.0).astype(BF16)
    upper = jnp.concatenate([g00[...], g01[...]], 1)
    lower = jnp.concatenate([g01[...].T, g11[...]], 1)
    gram = jnp.concatenate([upper, lower], 0)
    high, low = split_two(gram)
    by_row = jnp.dot(pick, high, preferred_element_type=F32)
    by_row += jnp.dot(pick, low, preferred_element_type=F32)
    high, low = split_two(by_row)
    out = nt(high, pick) + nt(low, pick)
    high, low = split_two(gram[ROWS : ROWS + 16, :])
    return out, nt(high, pick) + nt(low, pick)


def main(snaps, fields, x_ref, valid_ref, exps_ref, codes_ref, gram_ref, cross_ref,
         xs, run, i0, i1, g00, g01, g11):
    sources = x_ref.shape[0]
    for s in range(sources):
        xs[s, : fields * snaps, :] = x_ref[s]
        xs[s, fields * snaps : (fields + 1) * snaps, :] = jnp.broadcast_to(
            valid_ref[...], (snaps, LANES)
        )
        for k in range(3):
            to = (fields + 1 + k) * snaps
            xs[s, to : to + snaps, :] = x_ref[s, (8 + k) * snaps : (9 + k) * snaps, :]
    for ref in (run, g00, g01, g11, i1):
        ref[...] = jnp.zeros_like(ref)
    first = xs[0, pl.ds(0, 8, stride=snaps), :]
    per = snaps // BLOCK

    def two(number, carry):
        source = number // (per // 2)
        start = pl.multiple_of((number % (per // 2)) * 2 * BLOCK, 2 * BLOCK)
        build(xs, first, run, i0, source, start, snaps)
        add_products(i1, g00, g01, g11)
        build(xs, first, run, i1, source, start + BLOCK, snaps)
        add_products(i0, g00, g01, g11)
        return carry

    lax.fori_loop(0, sources * per // 2, two, 0)
    add_products(i1, g00, g01, g11)
    gram_ref[...], cross_ref[...] = chosen(exps_ref, codes_ref, g00, g01, g11)


def shards(base_grid, sample_index, exponents):
    fields, snaps, cells = base_grid.shape
    points = sample_index.shape[0]
    terms = exponents.shape[0]
    time_devices = lax.axis_size("tm")
    point_devices = lax.axis_size("pts")
    own = points // time_devices
    index = sample_index.reshape(time_devices, own)
    index = jnp.pad(index, ((0, 0), (0, LANES - own)), constant_values=-1)
    valid = jnp.where(jnp.arange(LANES) < own, 1.0, 0.0).astype(F32).reshape(1, LANES)
    codes = jnp.asarray(np.array(CODES + [-1.0] * (FULL - ROWS), np.float32)).reshape(1, FULL)
    sampled = pl.pallas_call(
        sample,
        out_shape=jax.ShapeDtypeStruct((time_devices, fields * snaps, LANES), F32),
        compiler_params=pltpu.CompilerParams(vmem_limit_bytes=50 << 20),
    )(base_grid.reshape(fields * snaps, cells), index.reshape(1, time_devices * LANES))
    received = lax.all_to_all(sampled, "tm", 0, 0)
    gram_part, cross_part = pl.pallas_call(
        lambda *refs: main(snaps, fields, *refs),
        out_shape=(
            jax.ShapeDtypeStruct((terms, terms), F32),
            jax.ShapeDtypeStruct((16, terms), F32),
        ),
        scratch_shapes=[
            pltpu.VMEM((time_devices, SLOTS * snaps, LANES), F32),
            pltpu.VMEM((ROWS, LANES), F32),
            pltpu.VMEM((FULL, BLOCK * LANES), BF16),
            pltpu.VMEM((FULL, BLOCK * LANES), BF16),
            pltpu.VMEM((HALF, HALF), F32),
            pltpu.VMEM((HALF, HALF), F32),
            pltpu.VMEM((HALF, HALF), F32),
        ],
        compiler_params=pltpu.CompilerParams(vmem_limit_bytes=50 << 20),
    )(received, valid, exponents, codes)
    scale = 1.0 / (snaps * time_devices)
    norm = 1.0 / (snaps * time_devices * points * point_devices)
    gram = lax.psum_scatter(gram_part, "tm", scatter_dimension=1, tiled=True)
    gram = lax.psum_scatter(gram, "pts", scatter_dimension=0, tiled=True)
    row_span = terms // point_devices
    cross = lax.psum(cross_part[:TARGETS], ("tm", "pts"))
    cross = lax.dynamic_slice_in_dim(cross, lax.axis_index("pts") * row_span, row_span, 1)
    return gram * jnp.float32(norm * scale * scale), cross * jnp.float32(norm * scale)


def solution(mesh):
    return jax.shard_map(
        shards,
        mesh=mesh,
        in_specs=(P(None, "tm", "pts"), P("pts"), P()),
        out_specs=(P("pts", "tm"), P(None, "pts")),
        check_vma=False,
    )
```

time: 639 us -> 142 us (0.22)
  other arithmetic: 352 us -> 2.03 us
  local copies, waits for them, and re-layouts: 49.4 us -> 2.23 us
  matrix products: 44.3 us -> 0 us
  waiting for transfers between devices: 94.8 us -> 62.4 us
  starting transfers between devices: 31.3 us -> 4.25 us
  Pallas kernels: 0 us -> 16.7 us
  blocking collectives: 50.5 us -> 39.5 us
    another operation x8 -> x0, other arithmetic: 170 us -> none  [add_products(): running = jnp.cumsum(theta, axis=1)]
    reduce_sum x8 -> x0, other arithmetic: 162 us -> none  [add_totals(): jnp.sum(theta, axis=1)]
    psum x1 -> x0, waiting for transfers between devices: 90.4 us -> none  [shards(): gram_full, cross_full = lax.psum((gram_part, cross_part), ('tm', 'pts'))]
    reduce_scatter x0 -> x2, waiting for transfers between devices: none -> 50.8 us  [the longest x1 26 us: shards(): gram = lax.psum_scatter(gram_part, 'tm', scatter_dimension=1, tiled=True)]
    dot_general x16 -> x0, matrix products: 44.3 us -> none  [the longest x8 39 us: add_products(): lax.dot_general(integral, integral, contract, preferred_element_type=jnp....]
    ppermute x3 -> x0, starting transfers between devices: 31.3 us -> none  [passed_along(): return lax.ppermute(value, axis, pairs)]
    slice x8 -> x1, local copies, waits for them, and re-layouts: 19.1 us -> 0.01 us  [shards(): cross = lax.psum(cross_part[:TARGETS], ('tm', 'pts'))]
    pallas_call x0 -> x2, Pallas kernels: none -> 16.7 us  [the longest x1 14.4 us: shards(): pl.pallas_call(lambda *refs: main(snaps, fields, *refs), out_shape=(jax.S...]
  transfers between devices with their start and end apart: 4 -> 3, of which waited for: 3 -> 3; matrix products, arithmetic and copies ran while one was open for 1% -> 1% of each run, Pallas kernels for 0% -> 0%
where the time goes in v1:
time: 142 us; the launch traced here: 141 us
  waiting for transfers between devices  62.4 us (44%)
  blocking collectives  39.5 us (28%)
  Pallas kernels  16.7 us (12%)
  between operations  14.1 us (10%)
  starting transfers between devices  4.25 us (3%)
  local copies, waits for them, and re-layouts  2.23 us (2%)
  other arithmetic  2.03 us (1%)
    psum x1, blocking collectives, shards(): cross = lax.psum(cross_part[:TARGETS], ('tm', 'pts'))  39.5 us
    reduce_scatter x1, waiting for transfers between devices, shards(): gram = lax.psum_scatter(gram_part, 'tm', scatter_dimension=1, tiled=True)  26 us
    reduce_scatter x1, waiting for transfers between devices, shards(): gram = lax.psum_scatter(gram, 'pts', scatter_dimension=0, tiled=True)  24.8 us
    pallas_call x1, Pallas kernels, shards(): pl.pallas_call(lambda *refs: main(snaps, fields, *refs), out_shape=(jax.S...  14.4 us
    all_to_all x1, waiting for transfers between devices, shards(): received = lax.all_to_all(sampled, 'tm', 0, 0)  11.5 us
    all_to_all x1, starting transfers between devices, shards(): received = lax.all_to_all(sampled, 'tm', 0, 0)  4.21 us
  transfers between devices with their start and end apart: 3, of which 3 were waited for; matrix products, arithmetic and copies ran while one was open for 1% of the time, Pallas kernels for 0%

profile of v1, /device:TPU:0, one launch (start us, length us, event | category | flops | bytes accessed | tf_op | source)
XLA Modules:
  0.0 141.1 jit_solution(15676744170470439729)
XLA Ops:
  7.2 0.0 copy-start
  7.2 1.4 copy-done
  8.6 0.0 copy-start.2
  8.6 0.7 copy-done.2
  9.3 0.0 copy-start.3
  9.3 0.0 copy-start.1
  9.3 2.3 %shard_map.59 = f32[4,384,128]{2,1,0:T(8,128)} custom-call(f32[384,1024]{1,0:T(8,128)S(1)} %bitcast.2, s32[1,512]{1,0:T(1,128)S(1)} %bitcast.3), custom_call_target="tpu_custom_call" | custom-call | tf_op jit(solution)/shard_map/pallas_call | solution.py:201
  11.6 4.2 %all-to-all-start = ((f32[4,384,128]{2,1,0:T(8,128)}), f32[4,384,128]{2,1,0:T(8,128)S(1)}, u32[]{:S(2)}, u32[]{:S(2)}) async-start(f32[4,384,128]{2,1,0:T(8,128)} %shard_map.59), calls=%async_computation | async-start | bytes 1572864 | tf_op jit(solution)/shard_map/all_to_all | solution.py:206
  15.8 0.0 reduce-scatter.3.cloned.1.call-start
  15.8 0.0 copy-done.3
  15.8 0.1 copy.6.refs_2_
  16.0 11.5 %all-to-all-done.refs_0_ = f32[4,384,128]{2,1,0:T(8,128)S(1)} async-done(((f32[4,384,128]{2,1,0:T(8,128)}), f32[4,384,128]{2,1,0:T(8,128)S(1)}, u32[]{:S(2)}, u32[]{:S(2)}) %all-to-all-start) | async-done | bytes 786464 | tf_op jit(solution)/shard_map/all_to_all | solution.py:206
  27.4 0.0 copy-done.1
  27.5 14.4 %shard_map.60 = (f32[512,512]{1,0:T(8,128)}, f32[16,512]{1,0:T(8,128)S(1)}) custom-call(f32[4,384,128]{2,1,0:T(8,128)S(1)} %all-to-all-done.refs_0_, f32[1,128]{1,0:T(1,128)S(1)} %compare_select_fusion.refs_1_, s32[512,12]{1,0:T(8,128)S(1)} %copy.6.refs_2_, f32[1,512]{1,0:T(1,128)S(1)} %copy-done.1), custom_call_target="tpu_custom_call" | custom-call | tf_op jit(solution)/shard_map/pallas_call | solution.py:207
  41.8 0.0 reduce-scatter.3.cloned.1.call-update
  41.8 0.0 reduce-scatter.5.cloned.1.call-start
  41.9 26.0 %reduce-scatter.3.cloned.1.call-done = f32[512,128]{1,0:T(8,128)} async-done(((f32[512,512]{1,0:T(8,128)}), f32[512,128]{1,0:T(8,128)}) %reduce-scatter.3.cloned.1.call-update) | async-done | bytes 262160 | tf_op jit(solution)/shard_map/reduce_scatter | solution.py:226
  67.9 0.0 reduce-scatter.5.cloned.1.call-update
  67.9 39.5 %psum.7 = f32[3,512]{1,0:T(4,128)S(1)} all-reduce(f32[3,512]{1,0:T(4,128)S(1)} %slice.3), channel_id=1, replica_groups=mesh['tm'=4,'pts'=8] {'tm','pts'}, use_global_device_ids=true, to_apply=%region_2.3 | all-reduce | flops 1536 | bytes 12288 | tf_op jit(solution)/shard_map/psum | solution.py:229
  107.5 0.7 dynamic-slice_multiply_fusion
  108.1 24.8 %reduce-scatter.5.cloned.1.call-done = f32[64,128]{1,0:T(8,128)} async-done(((f32[512,128]{1,0:T(8,128)}), f32[64,128]{1,0:T(8,128)}) %reduce-scatter.5.cloned.1.call-update) | async-done | bytes 32784 | tf_op jit(solution)/shard_map/reduce_scatter | solution.py:227
  132.9 1.4 broadcast_multiply_fusion
  (2 shorter events, 0.0 us)
Async XLA Ops:
  7.2 1.4 copy-start
  8.6 0.7 copy-start.2
  9.3 6.5 %copy-start.3 = (s32[512,12]{0,1:T(8,128)S(1)}, s32[512,12]{0,1:T(8,128)}, u32[]{:S(2)}) copy-start(s32[512,12]{0,1:T(8,128)} %param.6) | copy-start | bytes 73732
  9.3 18.2 %copy-start.1 = (f32[1,512]{1,0:T(1,128)S(1)}, f32[1,512]{1,0:T(1,128)}, u32[]{:S(2)}) copy-start(f32[1,512]{1,0:T(1,128)} %constant.24.refs_3_) | copy-start | bytes 6148
  11.6 15.9 %all-to-all-start = ((f32[4,384,128]{2,1,0:T(8,128)}), f32[4,384,128]{2,1,0:T(8,128)S(1)}, u32[]{:S(2)}, u32[]{:S(2)}) async-start(f32[4,384,128]{2,1,0:T(8,128)} %shard_map.59), calls=%async_computation | async-start | bytes 1572864 | tf_op jit(solution)/shard_map/all_to_all | solution.py:206
  15.8 52.1 %reduce-scatter.3.cloned.1.call-start = ((), (), s32[]{:S(2)}) async-start(), calls=%async_computation.3 | async-start | bytes 1310720 | tf_op jit(solution)/shard_map/reduce_scatter | solution.py:226
  41.8 91.1 %reduce-scatter.5.cloned.1.call-start = ((), (), s32[]{:S(2)}) async-start(), calls=%async_computation.4 | async-start | bytes 294912 | tf_op jit(solution)/shard_map/reduce_scatter | solution.py:227
Sparse Core Ops, SparseCore 0:
  42.0 25.8 reduce-scatter.2
  71.6 61.2 reduce-scatter.4

commit v2 on v1

--- a/solution.py
+++ b/solution.py
@@ -65,20 +65,15 @@
 HALF = FULL // 2
 
 
-def sample(grid_ref, index_ref, out_ref):
-    cells = grid_ref.shape[1]
-    width = index_ref.shape[1]
-    number = lax.broadcasted_iota(jnp.int32, (cells, width), 0)
-    hot = jnp.where(number == index_ref[...], 1.0, 0.0).astype(BF16)
+def sample(grid_ref, index):
+    number = lax.broadcasted_iota(jnp.int32, (grid_ref.shape[1], index.shape[1]), 0)
+    hot = jnp.where(number == index, 1.0, 0.0).astype(BF16)
     value = grid_ref[...]
-    high, rest = value.astype(BF16), None
-    rest = value - high.astype(F32)
-    middle, low = split_two(rest)
+    high = value.astype(BF16)
+    middle, low = split_two(value - high.astype(F32))
     out = jnp.dot(high, hot, preferred_element_type=F32)
     out += jnp.dot(middle, hot, preferred_element_type=F32)
-    out += jnp.dot(low, hot, preferred_element_type=F32)
-    for d in range(out_ref.shape[0]):
-        out_ref[d] = out[:, d * LANES : (d + 1) * LANES]
+    return out + jnp.dot(low, hot, preferred_element_type=F32)
 
 
 def build(xs, first, run, integral, source, start, snaps):
@@ -139,8 +134,9 @@
     g11[...] += nt(bottom, bottom)
 
 
-def chosen(exps_ref, codes_ref, g00, g01, g11):
+def choose(exps_ref, codes_ref, g00, g01, g11, part, rows, cols):
     terms, fields = exps_ref.shape
+    cores, xs_, zs, ys = part.shape[:4]
     power = lax.broadcasted_iota(jnp.int32, (1, fields), 1)
     weight = lax.shift_left(jnp.int32(1), 2 * power).astype(F32)
     code = jnp.sum(exps_ref[...].astype(F32) * weight, axis=1, keepdims=True)
@@ -154,81 +150,237 @@
     high, low = split_two(by_row)
     out = nt(high, pick) + nt(low, pick)
     high, low = split_two(gram[ROWS : ROWS + 16, :])
-    return out, nt(high, pick) + nt(low, pick)
-
-
-def main(snaps, fields, x_ref, valid_ref, exps_ref, codes_ref, gram_ref, cross_ref,
-         xs, run, i0, i1, g00, g01, g11):
-    sources = x_ref.shape[0]
-    for s in range(sources):
-        xs[s, : fields * snaps, :] = x_ref[s]
-        xs[s, fields * snaps : (fields + 1) * snaps, :] = jnp.broadcast_to(
-            valid_ref[...], (snaps, LANES)
+    for p in range(zs * ys):
+        own = pick[p * rows : (p + 1) * rows, :]
+        cross = (nt(high, own) + nt(low, own))[:8]
+        for c in range(cores * xs_):
+            place = (c % cores, c // cores, p // ys, p % ys)
+            block = out[p * rows : (p + 1) * rows, c * cols : (c + 1) * cols]
+            part[place + (slice(0, rows), slice(0, cols))] = block
+            part[place + (slice(rows, rows + 8), slice(0, rows))] = cross
+
+
+class Exchange:
+    def __init__(self, size, me, block, slots, sends, recvs, peer):
+        self.size, self.me, self.block, self.slots = size, me, block, slots
+        self.sends, self.recvs, self.peer = sends, recvs, peer
+
+    def others(self):
+        return [lax.rem(self.me + o, self.size) for o in range(1, self.size)]
+
+    def copy(self, member, slot):
+        return pltpu.make_async_remote_copy(
+            src_ref=self.block(member),
+            dst_ref=self.slots.at[slot],
+            send_sem=self.sends.at[member],
+            recv_sem=self.recvs.at[slot],
+            device_id=self.peer(member),
+            device_id_type=pl.DeviceIdType.MESH,
         )
+
+    def start(self):
+        for member in self.others():
+            self.copy(member, self.me).start()
+
+    def finish(self):
+        total = self.block(self.me)[...]
+        for member in self.others():
+            self.copy(member, member).wait_recv()
+            total = total + self.slots[member]
+        return total
+
+    def drain(self):
+        for member in self.others():
+            self.copy(member, member).wait_send()
+
+
+def main(snaps, fields, shape, gram_norm, cross_norm,
+         grid_ref, index_ref, valid_ref, exps_ref, codes_ref, gram_ref, cross_ref,
+         samp, xs, run, i0, i1, g00, g01, g11, part, r_core, s0, r_ax, s_a1, r_ay, s_a2, r_az,
+         r_by, s_b1, r_bx, s_b2, r_bz, sends, recvs, red_sends, red_recvs):
+    chips, depth, tall = shape
+    times = 2 * chips
+    rows, cols = gram_ref.shape
+    part_a = s_a1.shape[2]
+    tm, pts = lax.axis_index("tm"), lax.axis_index("pts")
+    x, core = tm // 2, lax.rem(tm, 2)
+    z, y = pts // tall, lax.rem(pts, tall)
+    mesh_id = pl.DeviceIdType.MESH
+
+    barrier = pltpu.get_barrier_semaphore()
+    for o in range(1, times):
+        pl.semaphore_signal(barrier, inc=1, device_id=(lax.rem(tm + o, times), pts), device_id_type=mesh_id)
+    for o in range(1, tall):
+        pl.semaphore_signal(barrier, inc=1, device_id=(tm, z * tall + lax.rem(y + o, tall)), device_id_type=mesh_id)
+    for o in range(1, depth):
+        pl.semaphore_signal(barrier, inc=1, device_id=(tm, lax.rem(z + o, depth) * tall + y), device_id_type=mesh_id)
+    pl.semaphore_wait(barrier, times - 1 + tall - 1 + depth - 1)
+
+    live = fields * snaps
+
+    def passed(to, source):
+        return pltpu.make_async_remote_copy(
+            src_ref=samp.at[to],
+            dst_ref=xs.at[source, pl.ds(0, live)],
+            send_sem=sends.at[to],
+            recv_sem=recvs.at[source],
+            device_id=(to, pts),
+            device_id_type=mesh_id,
+        )
+
+    for o in range(1, chips + 1):
+        there = lax.rem(x + o, chips)
+        out = sample(grid_ref, index_ref[there])
+        for c in range(2):
+            samp[2 * there + c] = out[:, c * LANES : (c + 1) * LANES]
+        if o < chips:
+            for c in range(2):
+                passed(2 * there + c, tm).start()
+    passed(2 * x + 1 - core, tm).start()
+    xs[tm, 0:live, :] = samp[tm]
+
+    for ref in (run, g00, g01, g11, i1, part):
+        ref[...] = jnp.zeros_like(ref)
+    per = snaps // BLOCK
+
+    def one_source(source, carry):
+        @pl.when(source != tm)
+        def _():
+            passed(source, source).wait_recv()
+
+        xs[source, live : live + snaps, :] = jnp.broadcast_to(valid_ref[...], (snaps, LANES))
         for k in range(3):
             to = (fields + 1 + k) * snaps
-            xs[s, to : to + snaps, :] = x_ref[s, (8 + k) * snaps : (9 + k) * snaps, :]
-    for ref in (run, g00, g01, g11, i1):
-        ref[...] = jnp.zeros_like(ref)
-    first = xs[0, pl.ds(0, 8, stride=snaps), :]
-    per = snaps // BLOCK
-
-    def two(number, carry):
-        source = number // (per // 2)
-        start = pl.multiple_of((number % (per // 2)) * 2 * BLOCK, 2 * BLOCK)
-        build(xs, first, run, i0, source, start, snaps)
-        add_products(i1, g00, g01, g11)
-        build(xs, first, run, i1, source, start + BLOCK, snaps)
-        add_products(i0, g00, g01, g11)
-        return carry
-
-    lax.fori_loop(0, sources * per // 2, two, 0)
+            xs[source, to : to + snaps, :] = xs[source, (8 + k) * snaps : (9 + k) * snaps, :]
+        first = xs[0, pl.ds(0, 8, stride=snaps), :]
+
+        def two(number, carry):
+            start = pl.multiple_of(number * 2 * BLOCK, 2 * BLOCK)
+            build(xs, first, run, i0, source, start, snaps)
+            add_products(i1, g00, g01, g11)
+            build(xs, first, run, i1, source, start + BLOCK, snaps)
+            add_products(i0, g00, g01, g11)
+            return carry
+
+        return lax.fori_loop(0, per // 2, two, carry)
+
+    lax.fori_loop(0, times, one_source, 0)
     add_products(i1, g00, g01, g11)
-    gram_ref[...], cross_ref[...] = chosen(exps_ref, codes_ref, g00, g01, g11)
+    for o in range(1, times):
+        to = lax.rem(tm + o, times)
+        passed(to, to).wait_send()
+    choose(exps_ref, codes_ref, g00, g01, g11, part, rows, cols)
+
+    def group(number, size, me, block, slots, peer):
+        return Exchange(size, me, block, slots, red_sends.at[number], red_recvs.at[number], peer)
+
+    def x_peer(j):
+        return (2 * j + core, pts)
+
+    def y_peer(j):
+        return (tm, z * tall + j)
+
+    def z_peer(j):
+        return (tm, j * tall + y)
+
+    e_core = group(0, 2, core, lambda j: part.at[j], r_core, lambda j: (2 * x + j, pts))
+    e_ax = group(1, chips, x, lambda j: s0.at[j, :, :, 0:part_a], r_ax, x_peer)
+    e_by = group(2, tall, y, lambda j: s0.at[:, :, j, part_a:], r_by, y_peer)
+    e_ay = group(3, tall, y, lambda j: s_a1.at[:, j], r_ay, y_peer)
+    e_bx = group(4, chips, x, lambda j: s_b1.at[j], r_bx, x_peer)
+    e_az = group(5, depth, z, lambda j: s_a2.at[j], r_az, z_peer)
+    e_bz = group(6, depth, z, lambda j: s_b2.at[j], r_bz, z_peer)
+    e_core.start()
+    s0[...] = e_core.finish()
+    e_ax.start()
+    e_by.start()
+    s_a1[...] = e_ax.finish()
+    e_ay.start()
+    s_b1[...] = e_by.finish()
+    e_bx.start()
+    s_a2[...] = e_ay.finish()
+    e_az.start()
+    s_b2[...] = e_bx.finish()
+    e_bz.start()
+    top = e_az.finish()
+    bottom = e_bz.finish()
+    total = jnp.concatenate([top, bottom], 0)
+    gram_ref[...] = total[:rows, :cols] * gram_norm
+    cross_ref[...] = total[rows : rows + TARGETS, :rows] * cross_norm
+    for exchange in (e_core, e_ax, e_by, e_ay, e_bx, e_az, e_bz):
+        exchange.drain()
 
 
 def shards(base_grid, sample_index, exponents):
     fields, snaps, cells = base_grid.shape
     points = sample_index.shape[0]
     terms = exponents.shape[0]
-    time_devices = lax.axis_size("tm")
+    times = lax.axis_size("tm")
     point_devices = lax.axis_size("pts")
-    own = points // time_devices
-    index = sample_index.reshape(time_devices, own)
+    chips = times // 2
+    depth = 4
+    tall = point_devices // depth
+    own = points // times
+    index = sample_index.reshape(times, own)
     index = jnp.pad(index, ((0, 0), (0, LANES - own)), constant_values=-1)
     valid = jnp.where(jnp.arange(LANES) < own, 1.0, 0.0).astype(F32).reshape(1, LANES)
     codes = jnp.asarray(np.array(CODES + [-1.0] * (FULL - ROWS), np.float32)).reshape(1, FULL)
-    sampled = pl.pallas_call(
-        sample,
-        out_shape=jax.ShapeDtypeStruct((time_devices, fields * snaps, LANES), F32),
-        compiler_params=pltpu.CompilerParams(vmem_limit_bytes=50 << 20),
-    )(base_grid.reshape(fields * snaps, cells), index.reshape(1, time_devices * LANES))
-    received = lax.all_to_all(sampled, "tm", 0, 0)
-    gram_part, cross_part = pl.pallas_call(
-        lambda *refs: main(snaps, fields, *refs),
+    scale = 1.0 / (snaps * times)
+    norm = 1.0 / (snaps * times * points * point_devices)
+    rows, cols = terms // point_devices, terms // times
+    high = rows + 8
+    part_a = -(-high // 16) * 8
+    part_b = high - part_a
+
+    def held(*extent):
+        return pltpu.VMEM(extent + (LANES,), F32)
+
+    most = max(chips, depth, tall, 2)
+    return pl.pallas_call(
+        lambda *refs: main(
+            snaps, fields, (chips, depth, tall), norm * scale * scale, norm * scale, *refs
+        ),
         out_shape=(
-            jax.ShapeDtypeStruct((terms, terms), F32),
-            jax.ShapeDtypeStruct((16, terms), F32),
+            jax.ShapeDtypeStruct((rows, cols), F32),
+            jax.ShapeDtypeStruct((TARGETS, rows), F32),
         ),
         scratch_shapes=[
-            pltpu.VMEM((time_devices, SLOTS * snaps, LANES), F32),
-            pltpu.VMEM((ROWS, LANES), F32),
+            held(times, fields * snaps),
+            held(times, SLOTS * snaps),
+            held(ROWS),
             pltpu.VMEM((FULL, BLOCK * LANES), BF16),
             pltpu.VMEM((FULL, BLOCK * LANES), BF16),
             pltpu.VMEM((HALF, HALF), F32),
             pltpu.VMEM((HALF, HALF), F32),
             pltpu.VMEM((HALF, HALF), F32),
+            held(2, chips, depth, tall, high),
+            held(2, chips, depth, tall, high),
+            held(chips, depth, tall, high),
+            held(chips, depth, tall, part_a),
+            held(depth, tall, part_a),
+            held(tall, depth, part_a),
+            held(depth, part_a),
+            held(depth, part_a),
+            held(tall, chips, depth, part_b),
+            held(chips, depth, part_b),
+            held(chips, depth, part_b),
+            held(depth, part_b),
+            held(depth, part_b),
+            pltpu.SemaphoreType.DMA((times,)),
+            pltpu.SemaphoreType.DMA((times,)),
+            pltpu.SemaphoreType.DMA((7, most)),
+            pltpu.SemaphoreType.DMA((7, most)),
         ],
-        compiler_params=pltpu.CompilerParams(vmem_limit_bytes=50 << 20),
-    )(received, valid, exponents, codes)
-    scale = 1.0 / (snaps * time_devices)
-    norm = 1.0 / (snaps * time_devices * points * point_devices)
-    gram = lax.psum_scatter(gram_part, "tm", scatter_dimension=1, tiled=True)
-    gram = lax.psum_scatter(gram, "pts", scatter_dimension=0, tiled=True)
-    row_span = terms // point_devices
-    cross = lax.psum(cross_part[:TARGETS], ("tm", "pts"))
-    cross = lax.dynamic_slice_in_dim(cross, lax.axis_index("pts") * row_span, row_span, 1)
-    return gram * jnp.float32(norm * scale * scale), cross * jnp.float32(norm * scale)
+        compiler_params=pltpu.CompilerParams(
+            collective_id=0, has_side_effects=True, vmem_limit_bytes=50 << 20
+        ),
+    )(
+        base_grid.reshape(fields * snaps, cells),
+        index.reshape(chips, 1, 2 * LANES),
+        valid,
+        exponents,
+        codes,
+    )
 
 
 def solution(mesh):

time: 142 us -> 51.2 us (0.36)
  waiting for transfers between devices: 62.4 us -> 0 us
  blocking collectives: 39.5 us -> 0 us
  Pallas kernels: 16.7 us -> 45.4 us
  between operations: 14.1 us -> 0.66 us
  starting transfers between devices: 4.25 us -> 0 us
  local copies, waits for them, and re-layouts: 2.23 us -> 4.85 us
  other arithmetic: 2.03 us -> 0.01 us
    reduce_scatter x2 -> x0, waiting for transfers between devices: 50.8 us -> none  [the longest x1 26 us: shards(): gram = lax.psum_scatter(gram_part, 'tm', scatter_dimension=1, tiled=True)]
    psum x1 -> x0, blocking collectives: 39.5 us -> none  [shards(): cross = lax.psum(cross_part[:TARGETS], ('tm', 'pts'))]
    pallas_call x2 -> x1, Pallas kernels: 16.7 us -> 45.4 us  [shards(): pl.pallas_call(lambda *refs: main(snaps, fields, (chips, depth, tall), no...]
    all_to_all x1 -> x0, waiting for transfers between devices: 11.5 us -> none  [shards(): received = lax.all_to_all(sampled, 'tm', 0, 0)]
    all_to_all x1 -> x0, starting transfers between devices: 4.21 us -> none  [shards(): received = lax.all_to_all(sampled, 'tm', 0, 0)]
    unnamed x9, local copies, waits for them, and re-layouts: 2.23 us -> 4.85 us
    mul x2 -> x0, other arithmetic: 2.02 us -> none  [the longest x1 1.37 us: shards(): gram * jnp.float32(norm * scale * scale)]
  transfers between devices with their start and end apart: 3 -> 0, of which waited for: 3 -> 0; matrix products, arithmetic and copies ran while one was open for 1% -> 0% of each run, Pallas kernels for 0% -> 0%
where the time goes in v2:
time: 51.2 us; the launch traced here: 51 us
  Pallas kernels  45.4 us (89%)
  local copies, waits for them, and re-layouts  4.85 us (9%)
  between operations  0.66 us (1%)
    pallas_call x1, Pallas kernels, shards(): pl.pallas_call(lambda *refs: main(snaps, fields, (chips, depth, tall), no...  45.4 us
    unnamed x9, local copies, waits for them, and re-layouts  4.85 us

profile of v2, /device:TPU:0, one launch (start us, length us, event | category | flops | bytes accessed | tf_op | source)
XLA Modules:
  0.0 51.0 jit_solution(12205953547477666714)
XLA Ops:
  0.6 0.9 %copy.6.refs_3_ = s32[512,12]{1,0:T(8,128)S(1)} copy(s32[512,12]{0,1:T(8,128)} %param.6) | data formatting | bytes 49152 | tf_op args[2]
  1.5 0.0 copy-start
  1.5 1.4 %copy-done = f32[12,32,1024]{2,1,0:T(8,128)S(1)} copy-done((f32[12,32,1024]{2,1,0:T(8,128)S(1)}, f32[12,32,1024]{2,1,0:T(8,128)}, u32[]{:S(2)}) %copy-start) | copy-done | bytes 1572888
  3.0 0.0 copy-start.1
  3.0 0.7 %copy-done.1 = s32[512]{0:T(512)S(1)} copy-done((s32[512]{0:T(512)S(1)}, s32[512]{0:T(512)}, u32[]{:S(2)}) %copy-start.1) | copy-done | bytes 2072
  3.6 0.0 copy-start.2
  3.6 0.7 %copy-done.2 = f32[1,512]{1,0:T(1,128)S(1)} copy-done((f32[1,512]{1,0:T(1,128)S(1)}, f32[1,512]{1,0:T(1,128)}, u32[]{:S(2)}) %copy-start.2) | copy-done | bytes 2072
  4.3 45.4 %shard_map.59 = (f32[64,128]{1,0:T(8,128)S(1)}, f32[3,64]{1,0:T(4,128)S(1)}) custom-call(f32[384,1024]{1,0:T(8,128)S(1)} %bitcast.2, s32[2,1,256]{2,1,0:T(1,128)S(1)} %bitcast.3, f32[1,128]{1,0:T(1,128)S(1)} %compare_select_fusion.refs_2_, s32[512,12]{1,0:T(8,128)S(1)} %copy.6.refs_3_, f32[1,512]{1,0:T(1,128)S(1)} %copy-done.2), custom_call_target="tpu_custom_call" | custom-call | tf_op jit(solution)/shard_map/pallas_call | solution.py:339
  49.8 0.6 %copy.9 = f32[64,128]{1,0:T(8,128)} copy(f32[64,128]{1,0:T(8,128)S(1)} %get-tuple-element.4) | data formatting | bytes 65536
  50.4 0.6 %copy.10 = f32[3,64]{1,0:T(4,128)} copy(f32[3,64]{1,0:T(4,128)S(1)} %get-tuple-element.5) | data formatting | bytes 1536
  (1 shorter events, 0.0 us)
Async XLA Ops:
  1.5 1.4 %copy-start = (f32[12,32,1024]{2,1,0:T(8,128)S(1)}, f32[12,32,1024]{2,1,0:T(8,128)}, u32[]{:S(2)}) copy-start(f32[12,32,1024]{2,1,0:T(8,128)} %param.4) | copy-start | bytes 4718596
  3.0 0.7 %copy-start.1 = (s32[512]{0:T(512)S(1)}, s32[512]{0:T(512)}, u32[]{:S(2)}) copy-start(s32[512]{0:T(512)} %param.5) | copy-start | bytes 6148
  3.6 0.7 %copy-start.2 = (f32[1,512]{1,0:T(1,128)S(1)}, f32[1,512]{1,0:T(1,128)}, u32[]{:S(2)}) copy-start(f32[1,512]{1,0:T(1,128)} %constant.10.refs_4_) | copy-start | bytes 6148

commit v3 on v2

--- a/solution.py
+++ b/solution.py
@@ -135,11 +135,12 @@
 
 
 def choose(exps_ref, codes_ref, g00, g01, g11, part, rows, cols):
-    terms, fields = exps_ref.shape
+    fields, terms = exps_ref.shape
     cores, xs_, zs, ys = part.shape[:4]
-    power = lax.broadcasted_iota(jnp.int32, (1, fields), 1)
+    power = lax.broadcasted_iota(jnp.int32, (fields, 1), 0)
     weight = lax.shift_left(jnp.int32(1), 2 * power).astype(F32)
-    code = jnp.sum(exps_ref[...].astype(F32) * weight, axis=1, keepdims=True)
+    code = jnp.sum(exps_ref[...].astype(F32) * weight, axis=0, keepdims=True)
+    code = jnp.broadcast_to(code, (8, terms)).T[:, :1]
     pick = jnp.where(code == codes_ref[...], 1.0, 0.0).astype(BF16)
     upper = jnp.concatenate([g00[...], g01[...]], 1)
     lower = jnp.concatenate([g01[...].T, g11[...]], 1)
@@ -194,9 +195,9 @@
             self.copy(member, member).wait_send()
 
 
-def main(snaps, fields, shape, gram_norm, cross_norm,
-         grid_ref, index_ref, valid_ref, exps_ref, codes_ref, gram_ref, cross_ref,
-         samp, xs, run, i0, i1, g00, g01, g11, part, r_core, s0, r_ax, s_a1, r_ay, s_a2, r_az,
+def main(snaps, fields, own, shape, gram_norm, cross_norm,
+         grid_in, index_in, exps_in, codes_in, gram_ref, cross_ref,
+         grid_ref, index_ref, exps_ref, codes_ref, loads, samp, xs, run, i0, i1, g00, g01, g11, part, r_core, s0, r_ax, s_a1, r_ay, s_a2, r_az,
          r_by, s_b1, r_bx, s_b2, r_bz, sends, recvs, red_sends, red_recvs):
     chips, depth, tall = shape
     times = 2 * chips
@@ -207,6 +208,10 @@
     z, y = pts // tall, lax.rem(pts, tall)
     mesh_id = pl.DeviceIdType.MESH
 
+    pairs = ((grid_in, grid_ref), (index_in, index_ref), (exps_in, exps_ref), (codes_in, codes_ref))
+    inputs = [pltpu.make_async_copy(a, b, loads.at[i]) for i, (a, b) in enumerate(pairs)]
+    for copy in inputs:
+        copy.start()
     barrier = pltpu.get_barrier_semaphore()
     for o in range(1, times):
         pl.semaphore_signal(barrier, inc=1, device_id=(lax.rem(tm + o, times), pts), device_id_type=mesh_id)
@@ -217,6 +222,8 @@
     pl.semaphore_wait(barrier, times - 1 + tall - 1 + depth - 1)
 
     live = fields * snaps
+    inputs[1].wait()
+    inputs[0].wait()
 
     def passed(to, source):
         return pltpu.make_async_remote_copy(
@@ -234,8 +241,12 @@
         for c in range(2):
             samp[2 * there + c] = out[:, c * LANES : (c + 1) * LANES]
         if o < chips:
-            for c in range(2):
-                passed(2 * there + c, tm).start()
+
+            @pl.when(core == 0)
+            def _():
+                for c in range(2):
+                    passed(2 * there + c, tm).start()
+
     passed(2 * x + 1 - core, tm).start()
     xs[tm, 0:live, :] = samp[tm]
 
@@ -243,12 +254,21 @@
         ref[...] = jnp.zeros_like(ref)
     per = snaps // BLOCK
 
+    valid = jnp.where(lax.broadcasted_iota(jnp.int32, (snaps, LANES), 1) < own, 1.0, 0.0).astype(F32)
+
     def one_source(source, carry):
+        @pl.when((source == 1) & (core == 1))
+        def _():
+            for o in range(1, chips):
+                there = lax.rem(x + o, chips)
+                for c in range(2):
+                    passed(2 * there + c, tm).start()
+
         @pl.when(source != tm)
         def _():
             passed(source, source).wait_recv()
 
-        xs[source, live : live + snaps, :] = jnp.broadcast_to(valid_ref[...], (snaps, LANES))
+        xs[source, live : live + snaps, :] = valid
         for k in range(3):
             to = (fields + 1 + k) * snaps
             xs[source, to : to + snaps, :] = xs[source, (8 + k) * snaps : (9 + k) * snaps, :]
@@ -269,6 +289,8 @@
     for o in range(1, times):
         to = lax.rem(tm + o, times)
         passed(to, to).wait_send()
+    inputs[2].wait()
+    inputs[3].wait()
     choose(exps_ref, codes_ref, g00, g01, g11, part, rows, cols)
 
     def group(number, size, me, block, slots, peer):
@@ -323,7 +345,6 @@
     own = points // times
     index = sample_index.reshape(times, own)
     index = jnp.pad(index, ((0, 0), (0, LANES - own)), constant_values=-1)
-    valid = jnp.where(jnp.arange(LANES) < own, 1.0, 0.0).astype(F32).reshape(1, LANES)
     codes = jnp.asarray(np.array(CODES + [-1.0] * (FULL - ROWS), np.float32)).reshape(1, FULL)
     scale = 1.0 / (snaps * times)
     norm = 1.0 / (snaps * times * points * point_devices)
@@ -338,13 +359,19 @@
     most = max(chips, depth, tall, 2)
     return pl.pallas_call(
         lambda *refs: main(
-            snaps, fields, (chips, depth, tall), norm * scale * scale, norm * scale, *refs
+            snaps, fields, own, (chips, depth, tall), norm * scale * scale, norm * scale, *refs
         ),
         out_shape=(
             jax.ShapeDtypeStruct((rows, cols), F32),
             jax.ShapeDtypeStruct((TARGETS, rows), F32),
         ),
+        in_specs=[pl.BlockSpec(memory_space=pltpu.HBM)] * 4,
         scratch_shapes=[
+            pltpu.VMEM((fields * snaps, cells), F32),
+            pltpu.VMEM((chips, 1, 2 * LANES), jnp.int32),
+            pltpu.VMEM((fields, terms), jnp.int32),
+            pltpu.VMEM((1, FULL), F32),
+            pltpu.SemaphoreType.DMA((4,)),
             held(times, fields * snaps),
             held(times, SLOTS * snaps),
             held(ROWS),
@@ -372,13 +399,12 @@
             pltpu.SemaphoreType.DMA((7, most)),
         ],
         compiler_params=pltpu.CompilerParams(
-            collective_id=0, has_side_effects=True, vmem_limit_bytes=50 << 20
+            collective_id=0, has_side_effects=True, vmem_limit_bytes=64 << 20
         ),
     )(
         base_grid.reshape(fields * snaps, cells),
         index.reshape(chips, 1, 2 * LANES),
-        valid,
-        exponents,
+        exponents.T,
         codes,
     )
 

time: 51.2 us -> 48.2 us (0.941)
  local copies, waits for them, and re-layouts: 4.85 us -> 2.62 us
  Pallas kernels: 45.4 us -> 44.8 us
    unnamed x9 -> x2, local copies, waits for them, and re-layouts: 4.85 us -> 2.62 us
    pallas_call x1, Pallas kernels: 45.4 us -> 44.8 us  [shards(): pl.pallas_call(lambda *refs: main(snaps, fields, own, (chips, depth, tall...]
where the time goes in v3:
time: 48.2 us; the launch traced here: 48 us
  Pallas kernels  44.8 us (93%)
  local copies, waits for them, and re-layouts  2.62 us (5%)
  between operations  0.64 us (1%)
    pallas_call x1, Pallas kernels, shards(): pl.pallas_call(lambda *refs: main(snaps, fields, own, (chips, depth, tall...  44.8 us
    unnamed x2, local copies, waits for them, and re-layouts  2.62 us

profile of v3, /device:TPU:0, one launch (start us, length us, event | category | flops | bytes accessed | tf_op | source)
XLA Modules:
  0.0 48.0 jit_solution(13957715999460630585)
XLA Ops:
  0.6 44.8 %shard_map.59 = (f32[64,128]{1,0:T(8,128)}, f32[3,64]{1,0:T(4,128)}) custom-call(f32[384,1024]{1,0:T(8,128)} %bitcast.3, s32[2,1,256]{2,1,0:T(1,128)} %bitcast.5, s32[12,512]{1,0:T(8,128)} %bitcast.4, f32[1,512]{1,0:T(1,128)} %constant.4.refs_3_), custom_call_target="tpu_custom_call" | custom-call | tf_op jit(solution)/shard_map/pallas_call | solution.py:360
  45.4 1.4 %copy.8 = f32[64,128]{1,0:T(8,128)} copy(f32[64,128]{1,0:T(8,128)} %get-tuple-element.4) | data formatting | bytes 65536
  46.8 1.2 %copy.9 = f32[3,64]{1,0:T(4,128)} copy(f32[3,64]{1,0:T(4,128)} %get-tuple-element.5) | data formatting | bytes 1536

commit v4 on v3

--- a/solution.py
+++ b/solution.py
@@ -305,16 +305,23 @@
     def z_peer(j):
         return (tm, j * tall + y)
 
-    e_core = group(0, 2, core, lambda j: part.at[j], r_core, lambda j: (2 * x + j, pts))
+    def core_peer(j):
+        return (2 * x + j, pts)
+
+    upper, lower = slice(0, part_a), slice(part_a, part.shape[4])
+    e_ca = group(0, 2, core, lambda j: part.at[j, :, :, :, upper], r_core.at[:, :, :, :, upper], core_peer)
+    e_cb = group(7, 2, core, lambda j: part.at[j, :, :, :, lower], r_core.at[:, :, :, :, lower], core_peer)
     e_ax = group(1, chips, x, lambda j: s0.at[j, :, :, 0:part_a], r_ax, x_peer)
     e_by = group(2, tall, y, lambda j: s0.at[:, :, j, part_a:], r_by, y_peer)
     e_ay = group(3, tall, y, lambda j: s_a1.at[:, j], r_ay, y_peer)
     e_bx = group(4, chips, x, lambda j: s_b1.at[j], r_bx, x_peer)
     e_az = group(5, depth, z, lambda j: s_a2.at[j], r_az, z_peer)
     e_bz = group(6, depth, z, lambda j: s_b2.at[j], r_bz, z_peer)
-    e_core.start()
-    s0[...] = e_core.finish()
+    e_ca.start()
+    e_cb.start()
+    s0[:, :, :, upper] = e_ca.finish()
     e_ax.start()
+    s0[:, :, :, lower] = e_cb.finish()
     e_by.start()
     s_a1[...] = e_ax.finish()
     e_ay.start()
@@ -329,7 +336,7 @@
     total = jnp.concatenate([top, bottom], 0)
     gram_ref[...] = total[:rows, :cols] * gram_norm
     cross_ref[...] = total[rows : rows + TARGETS, :rows] * cross_norm
-    for exchange in (e_core, e_ax, e_by, e_ay, e_bx, e_az, e_bz):
+    for exchange in (e_ca, e_cb, e_ax, e_by, e_ay, e_bx, e_az, e_bz):
         exchange.drain()
 
 
@@ -395,8 +402,8 @@
             held(depth, part_b),
             pltpu.SemaphoreType.DMA((times,)),
             pltpu.SemaphoreType.DMA((times,)),
-            pltpu.SemaphoreType.DMA((7, most)),
-            pltpu.SemaphoreType.DMA((7, most)),
+            pltpu.SemaphoreType.DMA((8, most)),
+            pltpu.SemaphoreType.DMA((8, most)),
         ],
         compiler_params=pltpu.CompilerParams(
             collective_id=0, has_side_effects=True, vmem_limit_bytes=64 << 20

time: 48.2 us -> 47.7 us (0.990)
  Pallas kernels: 44.8 us -> 44.2 us
    pallas_call x1, Pallas kernels: 44.8 us -> 44.2 us  [shards(): pl.pallas_call(lambda *refs: main(snaps, fields, own, (chips, depth, tall...]
where the time goes in v4:
time: 47.7 us; the launch traced here: 47.5 us
  Pallas kernels  44.2 us (93%)
  local copies, waits for them, and re-layouts  2.62 us (5%)
  between operations  0.64 us (1%)
    pallas_call x1, Pallas kernels, shards(): pl.pallas_call(lambda *refs: main(snaps, fields, own, (chips, depth, tall...  44.2 us
    unnamed x2, local copies, waits for them, and re-layouts  2.62 us

profile of v4, /device:TPU:0, one launch (start us, length us, event | category | flops | bytes accessed | tf_op | source)
XLA Modules:
  0.0 47.5 jit_solution(817749562030233169)
XLA Ops:
  0.6 44.2 %shard_map.59 = (f32[64,128]{1,0:T(8,128)}, f32[3,64]{1,0:T(4,128)}) custom-call(f32[384,1024]{1,0:T(8,128)} %bitcast.3, s32[2,1,256]{2,1,0:T(1,128)} %bitcast.5, s32[12,512]{1,0:T(8,128)} %bitcast.4, f32[1,512]{1,0:T(1,128)} %constant.4.refs_3_), custom_call_target="tpu_custom_call" | custom-call | tf_op jit(solution)/shard_map/pallas_call | solution.py:367
  44.9 1.4 %copy.8 = f32[64,128]{1,0:T(8,128)} copy(f32[64,128]{1,0:T(8,128)} %get-tuple-element.4) | data formatting | bytes 65536
  46.3 1.2 %copy.9 = f32[3,64]{1,0:T(4,128)} copy(f32[3,64]{1,0:T(4,128)} %get-tuple-element.5) | data formatting | bytes 1536
